TPU v7x, 512 devices: a whole 4x8x8 slice. The times are simulated.
512 devices in a mesh: page: 16 (over z, core), row: 32 (over x, y).
Axes of the slice: x: 4, y: 8, z: 8, core: 2. Of those that a mesh axis runs over, the one named last changes fastest.
Arguments:
- qkv_rows: bfloat16 [16, 2048, 3840], P('page', 'row'), may hold values from -12 to 12
- residual: bfloat16 [16, 2048, 1280], P('page', 'row'), may hold values from -40 to 40
- out_weight: bfloat16 [1280, 1280], P('page'), may hold values from -0.15625 to 0.15625
- norm_gain: float32 [1280], replicated, may hold values from 0.1 to 1.9
- merge_weight: bfloat16 [5120, 5120], P('row'), may hold values from -0.078125 to 0.078125
- merge_bias: float32 [5120], P('row'), may hold values from -3 to 3
- page_grid: int32 [16, 2], P('page'), may hold values from 2 to 256, as said below
Outputs:
- merged: bfloat16 [16, 5120, 512], P('page', 'row')
Inputs may be any that keep to these rules, and one draw needn't show every extreme that they name: `page_grid`: rows and columns are even; rows times columns is at most 2048, and one page of every draw has exactly 2048 live patches in 256 rows of 8 columns; columns are at least 8.
All inputs are finite; a program needn't handle non-finite values.
Results may differ from a plain program's by a relative error of at most 0.0049.
Values may be sent and summed in bfloat16 or wider, within the bound.
A program may use at most 64 MiB of HBM per device.

v0:
```python
import math
import jax
import jax.numpy as jnp
from jax import lax
from jax.sharding import PartitionSpec as P

D = 1280
HEADS = 16
HDIM = 80


def local(qkv_rows, residual, out_weight, norm_gain, merge_weight, merge_bias, page_grid):
    row_count = lax.axis_size("row")
    q_split = max(1, row_count // HEADS)
    head_groups = row_count // q_split
    width = D // head_groups
    heads_per = width // HDIM
    band_len = qkv_rows.shape[1]
    part_len = band_len // q_split
    local_qkv = qkv_rows[0]
    queries = local_qkv[:, :D]
    key_vals = jnp.concatenate(
        [
            local_qkv[:, D : 2 * D].reshape(band_len, head_groups, width),
            local_qkv[:, 2 * D :].reshape(band_len, head_groups, width),
        ],
        axis=2,
    )
    q_send = (
        queries.reshape(q_split, part_len, head_groups, width)
        .transpose(2, 0, 1, 3)
        .reshape(row_count, part_len, width)
    )
    kv_send = jnp.broadcast_to(
        key_vals.transpose(1, 0, 2)[:, None], (head_groups, q_split, band_len, 2 * width)
    )
    kv_send = kv_send.reshape(row_count, band_len, 2 * width)
    q_recv, kv_recv = (
        lax.all_to_all(q_send, "row", split_axis=0, concat_axis=1, tiled=True),
        lax.all_to_all(kv_send, "row", split_axis=0, concat_axis=1, tiled=True),
    )
    kv_local = kv_recv[0]
    positions = jnp.arange(row_count * band_len, dtype=jnp.int32)
    valid_len = page_grid[0, 0] * page_grid[0, 1]
    key_valid = positions < valid_len
    key_total = kv_local.shape[0]
    key_heads = kv_local[:, :width].reshape(key_total, heads_per, HDIM)
    value_heads = kv_local[:, width:].reshape(key_total, heads_per, HDIM)
    query_total = row_count * part_len
    q_block = math.gcd(query_total, 512)
    q_blocks = q_recv[0].reshape(query_total // q_block, q_block, heads_per, HDIM)
    root_dim = math.sqrt(HDIM)

    def attend(q_span):
        scores = (
            jnp.einsum("qhd,khd->hqk", q_span, key_heads, preferred_element_type=jnp.float32)
            / root_dim
        )
        scores = jnp.where(key_valid[None, None, :], scores, -1e30)
        peak = jnp.max(scores, axis=2, keepdims=True)
        weights = jnp.exp(scores - peak)
        total = jnp.sum(weights, axis=2, keepdims=True)
        mixed = (
            jnp.einsum(
                "hqk,khd->hqd",
                weights.astype(jnp.bfloat16),
                value_heads,
                preferred_element_type=jnp.float32,
            )
            / total
        )
        return mixed.transpose(1, 0, 2).reshape(q_span.shape[0], width).astype(jnp.bfloat16)

    attn_heads = lax.map(attend, q_blocks).reshape(row_count, part_len, width)
    returned = lax.all_to_all(attn_heads, "row", split_axis=0, concat_axis=0, tiled=True)
    attn = (
        returned.reshape(head_groups, q_split, part_len, width)
        .transpose(1, 2, 0, 3)
        .reshape(band_len, D)
    )
    projected = jnp.dot(
        attn,
        lax.all_gather(out_weight, "page", axis=0, tiled=True),
        preferred_element_type=jnp.float32,
    )
    hidden = residual[0].astype(jnp.float32) + projected
    normed = (
        hidden * lax.rsqrt(jnp.mean(hidden * hidden, axis=1, keepdims=True) + 1e-06) * norm_gain
    ).astype(jnp.bfloat16)
    rows_n = page_grid[0, 0]
    cols_n = page_grid[0, 1]
    group_total = band_len * row_count // 4
    slots = jnp.arange(group_total, dtype=jnp.int32)
    half_cols = cols_n // 2
    live = slots < rows_n // 2 * half_cols
    first = jnp.where(live, 2 * (slots // half_cols) * cols_n + 2 * (slots % half_cols), 0)
    corners = [first, first + 1, first + cols_n, first + cols_n + 1]
    local_units = merge_weight.shape[0]
    page_all = lax.all_gather(normed, "row", axis=0, tiled=True)
    merged_sum = jnp.zeros((local_units, group_total), jnp.float32)
    for corner in range(4):
        picked = jnp.take(page_all, corners[corner], axis=0)
        merged_sum = merged_sum + jnp.einsum(
            "md,gd->mg",
            merge_weight[:, corner * D : (corner + 1) * D],
            picked,
            preferred_element_type=jnp.float32,
        )
    merged = jax.nn.gelu(merged_sum + merge_bias[:, None], approximate=False)
    merged = jnp.where(live[None, :], merged, 0.0).astype(jnp.bfloat16)
    return merged[None]


def solution(mesh):
    in_specs = (
        P("page", "row", None),
        P("page", "row", None),
        P("page", None),
        P(),
        P("row", None),
        P("row"),
        P("page", None),
    )
    out_specs = P("page", "row", None)
    return jax.shard_map(local, mesh=mesh, in_specs=in_specs, out_specs=out_specs, check_vma=False)
```

profile of v0, /device:TPU:8, one launch (start us, length us, event | category | flops | bytes accessed | tf_op | source)
XLA Modules:
  0.0 219.9 jit_solution(7898743524473938593)
XLA Ops:
  6.5 0.7 all-gather.3.cloned.1.call-update
  7.3 1.1 fusion.101
  8.4 0.4 reshape.94
  8.8 0.8 copy.20
  9.5 10.2 %all-to-all-start = ((bf16[32,32,80]{2,1,0:T(8,128)(2,1)}), bf16[32,32,80]{2,1,0:T(8,128)(2,1)S(1)}, u32[]{:S(2)}, u32[]{:S(2)}) async-start(bf16[32,32,80]{2,1,0:T(8,128)(2,1)} %bitcast.5), calls=%async_computation | async-start | bytes 524288 | tf_op jit(solution)/shard_map/all_to_all | solution.py:39
  19.7 0.4 reshape.97
  20.1 0.4 reshape.96
  20.5 0.2 maximum_bitcast_fusion
  20.7 0.2 copy.21
  20.9 0.0 copy-start.2
  20.9 11.1 %all-to-all-done = bf16[32,32,80]{2,1,0:T(8,128)(2,1)S(1)} async-done(((bf16[32,32,80]{2,1,0:T(8,128)(2,1)}), bf16[32,32,80]{2,1,0:T(8,128)(2,1)S(1)}, u32[]{:S(2)}, u32[]{:S(2)}) %all-to-all-start) | async-done | bytes 163872 | tf_op jit(solution)/shard_map/all_to_all | solution.py:39
  32.0 1.1 broadcast_in_dim.56
  33.1 4.6 %all-to-all-start.1 = ((bf16[32,64,160]{2,1,0:T(8,128)(2,1)}), bf16[32,64,160]{2,1,0:T(8,128)(2,1)S(1)}, u32[]{:S(2)}, u32[]{:S(2)}) async-start(bf16[32,64,160]{2,1,0:T(8,128)(2,1)} %bitcast.8), calls=%async_computation.1 | async-start | bytes 2097152 | tf_op jit(solution)/shard_map/all_to_all | solution.py:40
  37.7 0.0 all-gather.5.cloned.1.call-start
  37.7 0.6 fusion.102
  39.5 0.1 copy.23
  39.7 25.7 %all-to-all-done.1 = bf16[32,64,160]{2,1,0:T(8,128)(2,1)S(1)} async-done(((bf16[32,64,160]{2,1,0:T(8,128)(2,1)}), bf16[32,64,160]{2,1,0:T(8,128)(2,1)S(1)}, u32[]{:S(2)}, u32[]{:S(2)}) %all-to-all-start.1) | async-done | bytes 655392 | tf_op jit(solution)/shard_map/all_to_all | solution.py:40
  65.4 0.3 fusion.100
  65.6 0.2 copy.27
  65.8 0.2 copy.28
  66.0 5.9 %while.11 = (s32[]{:T(128)}, bf16[2,512,80]{1,2,0:T(8,128)(2,1)S(1)}, bf16[2,512,1,80]{1,3,2,0:T(8,128)(2,1)S(1)}, bf16[2048,1,80]{0,2,1:T(8,128)(2,1)S(1)}, bf1...) while((s32[]{:T(128)}, bf16[2,512,80]{1,2,0:T(8,128)(2,1)S(1)}, ...), condition=%wide.region_3.4_spmd.clone, body=%wide.region_0.3_spmd.clone.sunk | while | flops 347161600 | bytes 13420641 | solution.py:74
  66.1 0.9 fusion.112
  67.0 0.9 fusion.113
  67.9 1.1 fusion.114
  69.0 0.9 fusion.112
  69.9 0.9 fusion.113
  70.9 1.1 fusion.114
  71.9 0.0 copy-start
  71.9 0.2 copy.24
  72.1 16.5 %all_to_all.23 = bf16[32,32,80]{2,1,0:T(8,128)(2,1)S(1)} all-to-all(bf16[32,32,80]{2,1,0:T(8,128)(2,1)S(1)} %bitcast.123), channel_id=1, replica_groups=mesh['page'=16,'row'=32] {'row'}, dimensions={0} | all-to-all | bytes 327680 | tf_op jit(solution)/shard_map/all_to_all | solution.py:75
  88.6 0.2 copy.30
  88.8 0.3 reshape.103
  89.1 0.0 all-gather.3.cloned.1.call-done
  89.1 2.7 %multiply_reduce_fusion = (f32[64]{0:T(128)S(1)}, f32[64,1280]{1,0:T(8,128)S(1)}) fusion(bf16[64,1280]{1,0:T(8,128)(2,1)S(1)} %reshape.103, bf16[1280,1280]{1,0:T(8,128)(2,1)} %all-gather.3.cloned.1.call-done, bf16[1,64,1280]{2,1,0:T(8,128)(2,1)S(1)} %copy-done), kind=kOutput, calls=%fused_computation.78 | convolution fusion | flops 210042816 | bytes 3932416 | tf_op jit(solution)/shard_map/dot_general | solution.py:81
  91.9 0.8 multiply_convert_fusion
  92.7 0.0 all-gather.5.cloned.1.call-update
  98.1 0.1 compare_select_fusion.3
  98.2 0.1 compare_and_fusion.2
  98.4 0.8 compare_and_fusion
  99.2 83.0 %all-gather.5.cloned.1.call-done = bf16[2048,1280]{1,0:T(8,128)(2,1)} async-done(((bf16[64,1280]{1,0:T(8,128)(2,1)}), bf16[2048,1280]{1,0:T(8,128)(2,1)}) %all-gather.5.cloned.1.call-update) | async-done | bytes 5242896 | tf_op jit(solution)/shard_map/all_gather | solution.py:99
  182.2 6.3 %gather_fusion.1 = bf16[512,1280]{1,0:T(8,128)(2,1)S(1)} fusion(bf16[2048,1280]{1,0:T(8,128)(2,1)} %all-gather.5.cloned.1.call-done, s32[1024]{0:T(1024)S(1)} %pad_clamp_fusion.2), kind=kCustom, calls=%fused_computation.1.clone | custom fusion | bytes 2623488 | tf_op jit(solution)/shard_map/jit(_take)/gather | solution.py:102
  188.5 0.7 fusion.32
  189.1 6.3 %gather_fusion = bf16[512,1280]{1,0:T(8,128)(2,1)S(1)} fusion(bf16[2048,1280]{1,0:T(8,128)(2,1)} %all-gather.5.cloned.1.call-done, s32[1024]{0:T(1024)S(1)} %pad_clamp_fusion.3), kind=kCustom, calls=%fused_computation.clone | custom fusion | bytes 2623488 | tf_op jit(solution)/shard_map/jit(_take)/gather | solution.py:102
  195.4 1.4 fusion.40
  196.8 6.3 %gather_fusion.2 = bf16[512,1280]{1,0:T(8,128)(2,1)S(1)} fusion(bf16[2048,1280]{1,0:T(8,128)(2,1)} %all-gather.5.cloned.1.call-done, s32[1024]{0:T(1024)S(1)} %pad_clamp_fusion.1), kind=kCustom, calls=%fused_computation.2.clone | custom fusion | bytes 2623488 | tf_op jit(solution)/shard_map/jit(_take)/gather | solution.py:102
  203.1 1.6 fusion.43
  204.8 6.3 %gather_fusion.3 = bf16[512,1280]{1,0:T(8,128)(2,1)S(1)} fusion(bf16[2048,1280]{1,0:T(8,128)(2,1)} %all-gather.5.cloned.1.call-done, s32[1024]{0:T(1024)S(1)} %pad_clamp_fusion), kind=kCustom, calls=%fused_computation.3.clone | custom fusion | bytes 2623488 | tf_op jit(solution)/shard_map/jit(_take)/gather | solution.py:102
  211.1 2.0 fusion.83
  (18 shorter events, 0.1 us)
Async XLA Ops:
  6.5 82.6 %all-gather.3.cloned.1.call-start = ((), (), s32[]{:S(2)}) async-start(), calls=%async_computation.3 | async-start | bytes 3481600 | tf_op jit(solution)/shard_map/all_gather | solution.py:83
  9.5 22.5 %all-to-all-start = ((bf16[32,32,80]{2,1,0:T(8,128)(2,1)}), bf16[32,32,80]{2,1,0:T(8,128)(2,1)S(1)}, u32[]{:S(2)}, u32[]{:S(2)}) async-start(bf16[32,32,80]{2,1,0:T(8,128)(2,1)} %bitcast.5), calls=%async_computation | async-start | bytes 524288 | tf_op jit(solution)/shard_map/all_to_all | solution.py:39
  20.9 16.8 %copy-start.2 = (s32[1,2]{1,0:T(1,128)S(1)}, s32[1,2]{1,0:T(1,128)}, u32[]{:S(2)}) copy-start(s32[1,2]{1,0:T(1,128)} %param.17) | copy-start | bytes 28
  33.1 32.3 %all-to-all-start.1 = ((bf16[32,64,160]{2,1,0:T(8,128)(2,1)}), bf16[32,64,160]{2,1,0:T(8,128)(2,1)S(1)}, u32[]{:S(2)}, u32[]{:S(2)}) async-start(bf16[32,64,160]{2,1,0:T(8,128)(2,1)} %bitcast.8), calls=%async_computation.1 | async-start | bytes 2097152 | tf_op jit(solution)/shard_map/all_to_all | solution.py:40
  37.7 144.5 %all-gather.5.cloned.1.call-start = ((), (), s32[]{:S(2)}) async-start(), calls=%async_computation.4 | async-start | bytes 5406720 | tf_op jit(solution)/shard_map/all_gather | solution.py:99
  71.9 17.2 %copy-start = (bf16[1,64,1280]{2,1,0:T(8,128)(2,1)S(1)}, bf16[1,64,1280]{2,1,0:T(8,128)(2,1)}, u32[]{:S(2)}) copy-start(bf16[1,64,1280]{2,1,0:T(8,128)(2,1)} %param.12) | copy-start | bytes 491524
  89.1 2.8 %copy-start.1 = (f32[1280]{0:T(1024)S(1)}, f32[1280]{0:T(1024)}, u32[]{:S(2)}) copy-start(f32[1280]{0:T(1024)} %param.14) | copy-start | bytes 15364
  99.2 89.3 %copy-start.3 = (bf16[160,5120]{1,0:T(8,128)(2,1)S(1)}, bf16[160,5120]{1,0:T(8,128)(2,1)}, u32[]{:S(2)}) copy-start(bf16[160,5120]{1,0:T(8,128)(2,1)} %param.15) | copy-start | bytes 4915204
  204.8 6.3 %copy-start.4 = (f32[160]{0:T(256)S(1)}, f32[160]{0:T(256)}, u32[]{:S(2)}) copy-start(f32[160]{0:T(256)} %param.16) | copy-start | bytes 1924
Sparse Core Ops, SparseCore 0:
  9.5 49.1 all-gather.2
  92.8 89.3 all-gather.4
where the time goes:
time: 221 us; the launch traced here: 220 us
  waiting for transfers between devices  121 us (55%)
  local copies, waits for them, and re-layouts  31.4 us (14%)
  between operations  20.3 us (9%)
  blocking collectives  16.5 us (7%)
  starting transfers between devices  14.8 us (7%)
  matrix products  12.4 us (6%)
  other arithmetic  3.99 us (2%)
    all_gather x1, waiting for transfers between devices, local(): page_all = lax.all_gather(normed, 'row', axis=0, tiled=True)  83 us
    all_to_all x1, waiting for transfers between devices, local(): lax.all_to_all(kv_send, 'row', split_axis=0, concat_axis=1, tiled=True)  25.7 us
    gather x4, local copies, waits for them, and re-layouts, local(): picked = jnp.take(page_all, corners[corner], axis=0)  25.1 us
    all_to_all x1, blocking collectives, local(): lax.all_to_all(attn_heads, 'row', split_axis=0, concat_axis=0, tiled=True)  16.5 us
    all_to_all x1, waiting for transfers between devices, local(): lax.all_to_all(q_send, 'row', split_axis=0, concat_axis=1, tiled=True)  11.1 us
    all_to_all x1, starting transfers between devices, local(): lax.all_to_all(q_send, 'row', split_axis=0, concat_axis=1, tiled=True)  10.2 us
    dot_general x4, matrix products, local(): jnp.einsum('md,gd->mg', merge_weight[:, corner * D:(corner + 1) * D], pic...  5.72 us
    all_to_all x1, starting transfers between devices, local(): lax.all_to_all(kv_send, 'row', split_axis=0, concat_axis=1, tiled=True)  4.56 us
  transfers between devices with their start and end apart: 4, of which 3 were waited for; matrix products, arithmetic and copies ran while one was open for 6% of the time, Pallas kernels for 0%

commit v1 on v0

--- a/solution.py
+++ b/solution.py
@@ -96,7 +96,9 @@
     first = jnp.where(live, 2 * (slots // half_cols) * cols_n + 2 * (slots % half_cols), 0)
     corners = [first, first + 1, first + cols_n, first + cols_n + 1]
     local_units = merge_weight.shape[0]
-    page_all = lax.all_gather(normed, "row", axis=0, tiled=True)
+    page_all = jnp.concatenate(
+        lax.all_to_all(jnp.stack([normed] * lax.axis_size("row")), "row", 0, 0), axis=0
+    )
     merged_sum = jnp.zeros((local_units, group_total), jnp.float32)
     for corner in range(4):
         picked = jnp.take(page_all, corners[corner], axis=0)

time: 221 us -> 257 us (1.16)
  the two profiles are of different devices: /device:TPU:8 before, /device:TPU:72 now
where the time goes in v1:
time: 257 us; the launch traced here: 256 us
  waiting for transfers between devices  148 us (58%)
  local copies, waits for them, and re-layouts  36.1 us (14%)
  between operations  20.6 us (8%)
  starting transfers between devices  19.6 us (8%)
  blocking collectives  16.5 us (6%)
  matrix products  12.2 us (5%)
  other arithmetic  3.31 us (1%)
    all_to_all x1, waiting for transfers between devices, local(): lax.all_to_all(jnp.stack([normed] * lax.axis_size('row')), 'row', 0, 0)  110 us
    gather x4, local copies, waits for them, and re-layouts, local(): picked = jnp.take(page_all, corners[corner], axis=0)  26.7 us
    all_to_all x1, waiting for transfers between devices, local(): lax.all_to_all(kv_send, 'row', split_axis=0, concat_axis=1, tiled=True)  25.7 us
    all_to_all x1, blocking collectives, local(): lax.all_to_all(attn_heads, 'row', split_axis=0, concat_axis=0, tiled=True)  16.5 us
    all_to_all x1, waiting for transfers between devices, local(): lax.all_to_all(q_send, 'row', split_axis=0, concat_axis=1, tiled=True)  11.1 us
    all_to_all x1, starting transfers between devices, local(): lax.all_to_all(q_send, 'row', split_axis=0, concat_axis=1, tiled=True)  10.2 us
    dot_general x4, matrix products, local(): jnp.einsum('md,gd->mg', merge_weight[:, corner * D:(corner + 1) * D], pic...  5.51 us
  transfers between devices with their start and end apart: 4, of which 3 were waited for; matrix products, arithmetic and copies ran while one was open for 5% of the time, Pallas kernels for 0%

profile of v1, /device:TPU:72, one launch (start us, length us, event | category | flops | bytes accessed | tf_op | source)
XLA Modules:
  0.0 256.1 jit_solution(12301334023636167300)
XLA Ops:
  6.5 0.7 all-gather.2.cloned.1.call-update
  7.3 1.1 fusion.101
  8.4 0.4 reshape.99
  8.8 0.8 copy.20
  9.5 10.2 %all-to-all-start = ((bf16[32,32,80]{2,1,0:T(8,128)(2,1)}), bf16[32,32,80]{2,1,0:T(8,128)(2,1)S(1)}, u32[]{:S(2)}, u32[]{:S(2)}) async-start(bf16[32,32,80]{2,1,0:T(8,128)(2,1)} %bitcast.5), calls=%async_computation | async-start | bytes 524288 | tf_op jit(solution)/shard_map/all_to_all | solution.py:39
  19.7 0.4 reshape.102
  20.1 0.4 reshape.101
  20.5 0.2 maximum_bitcast_fusion
  20.7 0.2 copy.21
  20.9 11.1 %all-to-all-done = bf16[32,32,80]{2,1,0:T(8,128)(2,1)S(1)} async-done(((bf16[32,32,80]{2,1,0:T(8,128)(2,1)}), bf16[32,32,80]{2,1,0:T(8,128)(2,1)S(1)}, u32[]{:S(2)}, u32[]{:S(2)}) %all-to-all-start) | async-done | bytes 163872 | tf_op jit(solution)/shard_map/all_to_all | solution.py:39
  32.0 1.1 broadcast_in_dim.56
  33.1 4.6 %all-to-all-start.1 = ((bf16[32,64,160]{2,1,0:T(8,128)(2,1)}), bf16[32,64,160]{2,1,0:T(8,128)(2,1)S(1)}, u32[]{:S(2)}, u32[]{:S(2)}) async-start(bf16[32,64,160]{2,1,0:T(8,128)(2,1)} %bitcast.8), calls=%async_computation.1 | async-start | bytes 2097152 | tf_op jit(solution)/shard_map/all_to_all | solution.py:40
  37.7 0.6 fusion.102
  39.5 0.1 copy.23
  39.7 25.7 %all-to-all-done.1 = bf16[32,64,160]{2,1,0:T(8,128)(2,1)S(1)} async-done(((bf16[32,64,160]{2,1,0:T(8,128)(2,1)}), bf16[32,64,160]{2,1,0:T(8,128)(2,1)S(1)}, u32[]{:S(2)}, u32[]{:S(2)}) %all-to-all-start.1) | async-done | bytes 655392 | tf_op jit(solution)/shard_map/all_to_all | solution.py:40
  65.4 0.3 fusion.100
  65.6 0.2 copy.27
  65.8 0.2 copy.28
  66.0 5.9 %while.11 = (s32[]{:T(128)}, bf16[2,512,80]{1,2,0:T(8,128)(2,1)S(1)}, bf16[2,512,1,80]{1,3,2,0:T(8,128)(2,1)S(1)}, bf16[2048,1,80]{0,2,1:T(8,128)(2,1)S(1)}, bf1...) while((s32[]{:T(128)}, bf16[2,512,80]{1,2,0:T(8,128)(2,1)S(1)}, ...), condition=%wide.region_3.4_spmd.clone, body=%wide.region_0.3_spmd.clone.sunk | while | flops 347161600 | bytes 13420641 | solution.py:74
  66.1 0.9 fusion.112
  67.0 0.9 fusion.113
  67.9 1.1 fusion.114
  69.0 0.9 fusion.112
  69.9 0.9 fusion.113
  70.9 1.1 fusion.114
  71.9 0.2 copy.24
  72.1 16.5 %all_to_all.28 = bf16[32,32,80]{2,1,0:T(8,128)(2,1)S(1)} all-to-all(bf16[32,32,80]{2,1,0:T(8,128)(2,1)S(1)} %bitcast.124), channel_id=1, replica_groups=mesh['page'=16,'row'=32] {'row'}, dimensions={0} | all-to-all | bytes 327680 | tf_op jit(solution)/shard_map/all_to_all | solution.py:75
  88.7 0.2 copy.30
  88.8 0.3 reshape.108
  89.1 0.0 all-gather.2.cloned.1.call-done
  89.1 2.7 %multiply_reduce_fusion = (f32[64]{0:T(128)S(1)}, f32[64,1280]{1,0:T(8,128)S(1)}) fusion(bf16[64,1280]{1,0:T(8,128)(2,1)S(1)} %reshape.108, bf16[1280,1280]{1,0:T(8,128)(2,1)} %all-gather.2.cloned.1.call-done, bf16[1,64,1280]{2,1,0:T(8,128)(2,1)S(1)} %copy-done.1), kind=kOutput, calls=%fused_computation.78 | convolution fusion | flops 210042816 | bytes 3932416 | tf_op jit(solution)/shard_map/dot_general | solution.py:81
  91.9 0.1 multiply_convert_fusion
  92.0 2.9 %stack.2 = bf16[32,64,1280]{2,1,0:T(8,128)(2,1)} broadcast(bf16[64,1280]{1,0:T(8,128)(2,1)S(1)} %multiply_convert_fusion), dimensions={1,2} | broadcast | bytes 5406720 | tf_op jit(solution)/shard_map/stack | solution.py:100
  95.0 4.8 %all-to-all-start.3 = ((bf16[32,64,1280]{2,1,0:T(8,128)(2,1)}), bf16[32,64,1280]{2,1,0:T(8,128)(2,1)}, u32[]{:S(2)}, u32[]{:S(2)}) async-start(bf16[32,64,1280]{2,1,0:T(8,128)(2,1)} %stack.2), calls=%async_computation.3 | async-start | bytes 10485760 | tf_op jit(solution)/shard_map/all_to_all | solution.py:100
  105.5 0.1 compare_select_fusion.3
  105.6 0.1 compare_and_fusion.2
  105.8 0.8 compare_and_fusion
  106.6 110.3 %all-to-all-done.3 = bf16[32,64,1280]{2,1,0:T(8,128)(2,1)} async-done(((bf16[32,64,1280]{2,1,0:T(8,128)(2,1)}), bf16[32,64,1280]{2,1,0:T(8,128)(2,1)}, u32[]{:S(2)}, u32[]{:S(2)}) %all-to-all-start.3) | async-done | bytes 5242912 | tf_op jit(solution)/shard_map/all_to_all | solution.py:100
  216.9 7.1 %gather_fusion.1 = bf16[512,1280]{1,0:T(8,128)(2,1)} fusion(bf16[2048,1280]{1,0:T(8,128)(2,1)} %bitcast.15, s32[1024]{0:T(1024)S(1)} %pad_clamp_fusion.2), kind=kCustom, calls=%fused_computation.1.clone | custom fusion | bytes 2623488 | tf_op jit(solution)/shard_map/jit(_take)/gather | solution.py:104
  223.9 7.1 %gather_fusion = bf16[512,1280]{1,0:T(8,128)(2,1)} fusion(bf16[2048,1280]{1,0:T(8,128)(2,1)} %bitcast.15, s32[1024]{0:T(1024)S(1)} %pad_clamp_fusion.3), kind=kCustom, calls=%fused_computation.clone | custom fusion | bytes 2623488 | tf_op jit(solution)/shard_map/jit(_take)/gather | solution.py:104
  231.0 6.3 %gather_fusion.2 = bf16[512,1280]{1,0:T(8,128)(2,1)S(1)} fusion(bf16[2048,1280]{1,0:T(8,128)(2,1)} %bitcast.15, s32[1024]{0:T(1024)S(1)} %pad_clamp_fusion.1), kind=kCustom, calls=%fused_computation.2.clone | custom fusion | bytes 2623488 | tf_op jit(solution)/shard_map/jit(_take)/gather | solution.py:104
  237.3 6.3 %gather_fusion.3 = bf16[512,1280]{1,0:T(8,128)(2,1)S(1)} fusion(bf16[2048,1280]{1,0:T(8,128)(2,1)} %bitcast.15, s32[1024]{0:T(1024)S(1)} %pad_clamp_fusion), kind=kCustom, calls=%fused_computation.3.clone | custom fusion | bytes 2623488 | tf_op jit(solution)/shard_map/jit(_take)/gather | solution.py:104
  243.6 2.2 fusion.32
  245.8 0.1 copy-done.4
  245.9 0.7 fusion.40
  246.6 0.7 fusion.43
  247.3 0.0 copy-done.5
  247.3 2.0 fusion.83
  (20 shorter events, 0.1 us)
Async XLA Ops:
  6.5 82.6 %all-gather.2.cloned.1.call-start = ((), (), s32[]{:S(2)}) async-start(), calls=%async_computation.4 | async-start | bytes 3481600 | tf_op jit(solution)/shard_map/all_gather | solution.py:83
  9.5 22.5 %all-to-all-start = ((bf16[32,32,80]{2,1,0:T(8,128)(2,1)}), bf16[32,32,80]{2,1,0:T(8,128)(2,1)S(1)}, u32[]{:S(2)}, u32[]{:S(2)}) async-start(bf16[32,32,80]{2,1,0:T(8,128)(2,1)} %bitcast.5), calls=%async_computation | async-start | bytes 524288 | tf_op jit(solution)/shard_map/all_to_all | solution.py:39
  20.9 16.8 %copy-start.3 = (s32[1,2]{1,0:T(1,128)S(1)}, s32[1,2]{1,0:T(1,128)}, u32[]{:S(2)}) copy-start(s32[1,2]{1,0:T(1,128)} %param.17) | copy-start | bytes 28
  33.1 32.3 %all-to-all-start.1 = ((bf16[32,64,160]{2,1,0:T(8,128)(2,1)}), bf16[32,64,160]{2,1,0:T(8,128)(2,1)S(1)}, u32[]{:S(2)}, u32[]{:S(2)}) async-start(bf16[32,64,160]{2,1,0:T(8,128)(2,1)} %bitcast.8), calls=%async_computation.1 | async-start | bytes 2097152 | tf_op jit(solution)/shard_map/all_to_all | solution.py:40
  71.9 17.2 %copy-start.1 = (bf16[1,64,1280]{2,1,0:T(8,128)(2,1)S(1)}, bf16[1,64,1280]{2,1,0:T(8,128)(2,1)}, u32[]{:S(2)}) copy-start(bf16[1,64,1280]{2,1,0:T(8,128)(2,1)} %param.12) | copy-start | bytes 491524
  89.1 2.8 %copy-start.2 = (f32[1280]{0:T(1024)S(1)}, f32[1280]{0:T(1024)}, u32[]{:S(2)}) copy-start(f32[1280]{0:T(1024)} %param.14) | copy-start | bytes 15364
  95.0 121.9 %all-to-all-start.3 = ((bf16[32,64,1280]{2,1,0:T(8,128)(2,1)}), bf16[32,64,1280]{2,1,0:T(8,128)(2,1)}, u32[]{:S(2)}, u32[]{:S(2)}) async-start(bf16[32,64,1280]{2,1,0:T(8,128)(2,1)} %stack.2), calls=%async_computation.3 | async-start | bytes 10485760 | tf_op jit(solution)/shard_map/all_to_all | solution.py:100
  243.6 2.2 copy-start
  243.6 2.3 copy-start.4
  246.6 0.7 copy-start.5
Sparse Core Ops, SparseCore 0:
  9.5 47.7 all-gather.1
